TPU v7x, 128 devices: a whole 4x4x4 slice. The times are simulated.
128 devices in a mesh: rows: 32 (over z, x, core), cent: 4 (over y).
Axes of the slice: x: 4, y: 4, z: 4, core: 2. Of those that a mesh axis runs over, the one named last changes fastest.
Arguments:
- embeds: bfloat16 [16384, 768], P('rows'), may hold values from -16 to 16
- centroids: bfloat16 [32768, 768], P('cent'), may hold values from -0.75 to 0.75
Outputs:
- resp: bfloat16 [16384, 32768], P('rows', 'cent')
- weights: float32 [32768], P(('cent', 'rows'))
- numer: float32 [32768, 768], P(('cent', 'rows'))
All inputs are finite; a program needn't handle non-finite values.
Results may differ from a plain program's by a relative error of at most 0.01.
Values may be sent and summed in bfloat16 or wider, within the bound.
A program may use at most 128 MiB of HBM per device.

v0:
```python
import jax
import jax.numpy as jnp
from jax import lax
from jax.sharding import PartitionSpec as P


def shards(embeds, centroids):
    scores = 10.0 * lax.dot_general(
        embeds, centroids, (((1,), (1,)), ((), ())), preferred_element_type=jnp.float32
    )
    local_peak = jnp.max(scores, axis=1)
    peak = lax.pmax(local_peak, "cent")
    expo = jnp.exp(scores - peak[:, None])
    total = lax.psum(jnp.sum(expo, axis=1), "cent")
    resp = (expo / total[:, None]).astype(jnp.bfloat16)
    term = lax.dot_general(
        resp, embeds, (((0,), (0,)), ((), ())), preferred_element_type=jnp.float32
    )
    col_sums = jnp.sum(resp, axis=0, dtype=jnp.float32)
    numer, weights = (
        lax.psum_scatter(term, "rows", scatter_dimension=0, tiled=True),
        lax.psum_scatter(col_sums, "rows", scatter_dimension=0, tiled=True),
    )
    return (resp, weights, numer)


def solution(mesh):
    return jax.shard_map(
        shards,
        mesh=mesh,
        in_specs=(P("rows", None), P("cent", None)),
        out_specs=(P("rows", "cent"), P(("cent", "rows")), P(("cent", "rows"), None)),
        check_vma=False,
    )
```

profile of v0, /device:TPU:1, one launch (start us, length us, event | category | flops | bytes accessed | tf_op | source)
XLA Modules:
  0.0 223.4 jit_solution(10783117544796611905)
XLA Ops:
  7.2 0.0 copy-start
  7.2 0.0 reduce-scatter.2.cloned.1.call-start
  7.2 1.1 copy-done
  8.3 14.8 %multiply_reduce_fusion = (f32[512]{0:T(512)S(1)}, f32[512,8192]{1,0:T(8,128)}) fusion(bf16[512,768]{1,0:T(8,128)(2,1)S(1)} %copy-done, bf16[8192,768]{1,0:T(8,128)(2,1)} %param.3), kind=kOutput, calls=%fused_computation.3 | convolution fusion | flops 6450839040 | bytes 30148608 | tf_op jit(solution)/shard_map/dot_general | solution.py:8
  23.1 9.5 %pmax.7 = f32[512]{0:T(512)S(1)} all-reduce(f32[512]{0:T(512)S(1)} %get-tuple-element.5), channel_id=1, replica_groups=mesh['rows'=32,'cent'=4] {'cent'}, use_global_device_ids=true, to_apply=%region_1.0 | all-reduce | flops 512 | bytes 4096 | tf_op jit(solution)/shard_map/pmax | solution.py:12
  32.6 8.6 %fusion = f32[512]{0:T(512)S(1)} fusion(f32[512,8192]{1,0:T(8,128)} %get-tuple-element.6, f32[512]{0:T(512)S(1)} %pmax.7), kind=kLoop, calls=%fused_computation.4 | loop fusion | flops 12582400 | bytes 16781312 | tf_op jit(solution)/shard_map/reduce_sum | solution.py:14
  41.2 6.0 %psum.7 = f32[512]{0:T(512)S(1)} all-reduce(f32[512]{0:T(512)S(1)} %fusion), channel_id=1, replica_groups=mesh['rows'=32,'cent'=4] {'cent'}, use_global_device_ids=true, to_apply=%region_3.0 | all-reduce | flops 512 | bytes 4096 | tf_op jit(solution)/shard_map/psum | solution.py:14
  47.2 7.9 %convert_reduce_fusion = (f32[8192]{0:T(1024)S(1)}, bf16[512,8192]{1,0:T(8,128)(2,1)S(1)}) fusion(f32[512]{0:T(512)S(1)} %psum.7, f32[512]{0:T(512)S(1)} %pmax.7, f32[512,8192]{1,0:T(8,128)} %get-tuple-element.6), kind=kLoop, calls=%fused_computation | loop fusion | flops 25157632 | bytes 25202688 | tf_op jit(solution)/shard_map/reduce_sum | solution.py:19
  55.2 0.0 copy-start.1
  55.2 3.4 %copy-done.1 = bf16[512,8192]{1,0:T(8,128)(2,1)} copy-done((bf16[512,8192]{1,0:T(8,128)(2,1)}, bf16[512,8192]{1,0:T(8,128)(2,1)S(1)}, u32[]{:S(2)}) %copy-start.1) | copy-done | bytes 8388632
  58.6 11.8 %fusion.1 = f32[8192,768]{1,0:T(8,128)} fusion(bf16[512,8192]{1,0:T(8,128)(2,1)S(1)} %get-tuple-element.4, bf16[512,768]{1,0:T(8,128)(2,1)S(1)} %copy-done), kind=kOutput, calls=%fused_computation.5 | convolution fusion | flops 6442450944 | bytes 34340864 | tf_op jit(solution)/shard_map/dot_general | solution.py:16
  70.4 0.0 copy-start.2
  70.4 0.0 reduce-scatter.2.cloned.1.call-update
  70.4 0.6 copy-done.2
  71.0 0.6 dynamic-slice
  72.3 127.0 %all-reduce = f32[8192]{0:T(1024)S(1)} all-reduce(f32[8192]{0:T(1024)S(1)} %get-tuple-element.3), channel_id=2, replica_groups=mesh['rows'=32,'cent'=4] {'rows'}, use_global_device_ids=true, to_apply=%region_5.0.clone | all-reduce | flops 8192 | bytes 65536
  199.3 0.6 dynamic-slice.1
  199.9 16.6 %reduce-scatter.2.cloned.1.call-done = f32[256,768]{1,0:T(8,128)} async-done(((f32[8192,768]{1,0:T(8,128)}), f32[256,768]{1,0:T(8,128)}) %reduce-scatter.2.cloned.1.call-update) | async-done | bytes 786448 | tf_op jit(solution)/shard_map/reduce_scatter | solution.py:21
Async XLA Ops:
  7.2 1.1 copy-start
  7.2 209.4 %reduce-scatter.2.cloned.1.call-start = ((), (), s32[]{:S(2)}) async-start(), calls=%async_computation.1 | async-start | bytes 25952256 | tf_op jit(solution)/shard_map/reduce_scatter | solution.py:21
  55.2 3.4 %copy-start.1 = (bf16[512,8192]{1,0:T(8,128)(2,1)}, bf16[512,8192]{1,0:T(8,128)(2,1)S(1)}, u32[]{:S(2)}) copy-start(bf16[512,8192]{1,0:T(8,128)(2,1)S(1)} %get-tuple-element.4) | copy-start | bytes 25165828
  70.4 0.7 copy-start.2
Sparse Core Ops, SparseCore 0:
  70.5 146.0 reduce-scatter.1
where the time goes:
time: 224 us; the launch traced here: 223 us
  blocking collectives  143 us (64%)
  matrix products  26.6 us (12%)
  waiting for transfers between devices  16.7 us (7%)
  other arithmetic  16.6 us (7%)
  between operations  14.7 us (7%)
  local copies, waits for them, and re-layouts  6.32 us (3%)
    unnamed x1, blocking collectives  127 us
    reduce_scatter x1, waiting for transfers between devices, shards(): lax.psum_scatter(term, 'rows', scatter_dimension=0, tiled=True)  16.6 us
    dot_general x1, matrix products, shards(): lax.dot_general(embeds, centroids, (((1,), (1,)), ((), ())), preferred_el...  14.8 us
    dot_general x1, matrix products, shards(): lax.dot_general(resp, embeds, (((0,), (0,)), ((), ())), preferred_element...  11.8 us
    pmax x1, blocking collectives, shards(): peak = lax.pmax(local_peak, 'cent')  9.53 us
    reduce_sum x1, other arithmetic, shards(): total = lax.psum(jnp.sum(expo, axis=1), 'cent')  8.62 us
    reduce_sum x1, other arithmetic, shards(): col_sums = jnp.sum(resp, axis=0, dtype=jnp.float32)  7.94 us
    unnamed x8, local copies, waits for them, and re-layouts  6.32 us
  transfers between devices with their start and end apart: 1, of which 1 were waited for; matrix products, arithmetic and copies ran while one was open for 1% of the time, Pallas kernels for 0%

commit v1 on v0

v1 whole, which is shorter than its diff:
```python
import functools
import math

import jax
import jax.numpy as jnp
from jax import lax
from jax.experimental import pallas as pl
from jax.experimental.pallas import tpu as pltpu
from jax.sharding import PartitionSpec as P

N, D, KL = 512, 768, 8192
NZ = NX = NY = 4
CH = 512
AHEAD = 6
NCH = KL // CH
OWN = 256
QF = 128
PIECE = 128
HALF = 128
PART = HALF + 16
VMEM_LIMIT = 40 << 20
SCALE = 10.0 * math.log2(math.e)
F32, BF16 = jnp.float32, jnp.bfloat16
MESH = pl.DeviceIdType.MESH
NT = (((1,), (1,)), ((), ()))
NN = (((1,), (0,)), ((), ()))


def position():
    r = lax.axis_index("rows")
    y = lax.axis_index("cent")
    return lax.div(r, 8), lax.rem(lax.div(r, 2), 4), lax.rem(r, 2), y


def device(dz, dx, dc, dy):
    z, x, c, y = position()
    z, x, y = lax.rem(z + dz, 4), lax.rem(x + dx, 4), lax.rem(y + dy, 4)
    return ((z * 4 + x) * 2 + lax.rem(c + dc, 2), y)


def first_pass(s_ref, m_ref, l_ref):
    for t in range(N // 32):
        rows = pl.ds(t * 32, 32)
        s = [s_ref[rows, pl.ds(g * 128, 128)] for g in range(CH // 128)]
        m = m_ref[rows, :]
        top = functools.reduce(jnp.maximum, s, m)
        total = l_ref[rows, :] * jnp.exp2((m - top) * SCALE)
        for g in s:
            total = total + jnp.exp2((g - top) * SCALE)
        m_ref[rows, :] = top
        l_ref[rows, :] = total


def slot(h, d, dc):
    return d * 2 + dc + 6 * h if d else dc


def to_axis(h, d, dc=0):
    return (0, d, dc, 0) if h == 0 else (d, 0, dc, 0)


PEERS = [(0, 0, 1, 0)] + [to_axis(h, d, dc) for h in range(2) for d in (1, 2, 3) for dc in range(2)]
YPEERS = [(0, 0, 0, dy) for dy in (1, 2, 3)]


def main_kernel(
    x_ref, c_hbm, resp_ref, numer_ref, w_ref,
    xs, xn, xf, cv, cc, s0, s1, m_ref, l_ref, acc, cols, stats, ystats, topc, invc, sb, rb,
    c_sem, cc_sem, own_s, own_r, near_s, near_r, far_s, far_r, ys, yr, pn_s, pn_r, pf_s, pf_r, ss, sr, yss, ysr, rs, rr,
):
    z, x, c, y = position()
    def c_copy(j):
        return pltpu.make_async_copy(c_hbm.at[pl.ds(j * CH, CH)], cv.at[j], c_sem.at[j])

    def cc_copy(h, q):
        owner = lax.rem(z + q, 4) * 8 + x * 2 + c if h == 0 else z * 8 + lax.rem(x + q, 4) * 2 + c
        start = pl.multiple_of(owner * OWN + h * HALF, HALF)
        return pltpu.make_async_copy(
            c_hbm.at[pl.ds(start, HALF)], cc.at[h, pl.ds(q * HALF, HALF)], cc_sem.at[h, q]
        )

    for j in range(AHEAD):
        c_copy(j).start()
    bar = pltpu.get_barrier_semaphore()
    for p in PEERS + YPEERS:
        pl.semaphore_signal(bar, inc=1, device_id=device(*p), device_id_type=MESH)
    m_ref[...] = jnp.full(m_ref.shape, -3e38, F32)
    l_ref[...] = jnp.zeros(l_ref.shape, F32)
    acc[...] = jnp.zeros(acc.shape, F32)
    cols[...] = jnp.zeros(cols.shape, F32)

    def scores(j, out):
        out[...] = lax.dot_general(x_ref[...], cv[j], NT, preferred_element_type=F32)

    c_copy(0).wait()
    scores(0, s0)

    def steps(a, b):
        @pl.loop(a, b)
        def _(i):
            c_copy(2 * i + 1).wait()
            c_copy(2 * i + 2).wait()
            scores(2 * i + 1, s1)
            first_pass(s0, m_ref, l_ref)
            scores(2 * i + 2, s0)
            first_pass(s1, m_ref, l_ref)

            @pl.when(i < (NCH - AHEAD) // 2)
            def _():
                c_copy(2 * i + AHEAD).start()
                c_copy(2 * i + AHEAD + 1).start()

    def remote(src, dst, send, recv, to):
        return pltpu.make_async_remote_copy(
            src_ref=src, dst_ref=dst, send_sem=send, recv_sem=recv, device_id=device(*to), device_id_type=MESH
        )

    sibling = remote(x_ref, xs, own_s, own_r, (0, 0, 1, 0))

    def near(h, k, side):
        rows = pl.ds(side * PIECE, PIECE)
        return remote(
            x_ref.at[pl.ds(k * PIECE, PIECE)], xn.at[h, k, rows],
            near_s.at[h, k, side], near_r.at[h, k, side], to_axis(h, 3 if side == 0 else 1),
        )

    def pass_near(h, k):
        return remote(
            xn.at[h, k, pl.ds(0, 2 * PIECE)], xn.at[h, k, pl.ds(2 * PIECE, 2 * PIECE)],
            pn_s.at[h, k], pn_r.at[h, k], (0, 0, 1, 0),
        )

    def quarter(q):
        return pl.ds(pl.multiple_of(QF * q, QF), QF)

    def far(h):
        rows = quarter(y)
        return remote(x_ref.at[rows], xf.at[h, 0, rows], far_s.at[h], far_r.at[h], to_axis(h, 2))

    def y_send(h, dy):
        rows = xf.at[h, 0, quarter(y)]
        return remote(rows, rows, ys.at[h, dy], yr.at[h, dy], (0, 0, 0, dy))

    def y_recv(h, dy):
        rows = xf.at[h, 0, quarter(lax.rem(y + 4 - dy, 4))]
        return remote(rows, rows, ys.at[h, dy], yr.at[h, dy], (0, 0, 0, dy))

    def pass_far(h, dy):
        rows = quarter(lax.rem(y + 4 - dy, 4))
        return remote(xf.at[h, 0, rows], xf.at[h, 1, rows], pf_s.at[h, dy], pf_r.at[h, dy], (0, 0, 1, 0))

    def stat_copy(h, d, dc):
        k = slot(h, d, dc)
        to = to_axis(h, (4 - d) % 4, dc)
        return remote(stats.at[0], stats.at[k], ss.at[k], sr.at[k], to)

    def ystat_copy(dy):
        return remote(ystats.at[0], ystats.at[dy], yss.at[dy], ysr.at[dy], (0, 0, 0, dy))

    def start_near(k):
        for side in range(2):
            for h in range(2):
                near(h, k, side).start()

    def take_near(k):
        for h in range(2):
            for side in range(2):
                near(h, k, side).wait_recv()
            pass_near(h, k).start()

    steps(0, 2)
    pl.semaphore_wait(bar, len(PEERS) + len(YPEERS))
    for h in range(2):
        far(h).start()
    sibling.start()
    steps(2, 4)
    start_near(0)
    for h in range(2):
        for q in range(4):
            cc_copy(h, q).start()
    steps(4, 6)
    start_near(1)
    steps(6, 7)
    c_copy(NCH - 1).wait()
    scores(NCH - 1, s1)
    first_pass(s0, m_ref, l_ref)
    first_pass(s1, m_ref, l_ref)

    m_t = jnp.transpose(m_ref[...])
    l_t = jnp.transpose(l_ref[...])
    top = jnp.max(m_t, axis=0, keepdims=True)
    total = jnp.sum(l_t * jnp.exp2((m_t - top) * SCALE), axis=0, keepdims=True)
    ystats[0, 0:8, :] = jnp.broadcast_to(top, (8, N))
    ystats[0, 8:16, :] = jnp.broadcast_to(total, (8, N))
    for dy in (1, 2, 3):
        ystat_copy(dy).start()
    for h in range(2):
        far(h).wait_recv()
        if h == 0:
            for dy in (1, 3, 2):
                y_send(h, dy).start()
        pass_far(h, 0).start()
    start_near(2)
    for dy in (1, 2, 3):
        ystat_copy(dy).wait_recv()
    tops = [ystats[dy, 0:8, :] for dy in range(4)]
    top = functools.reduce(jnp.maximum, tops)
    total = sum(ystats[dy, 8:16, :] * jnp.exp2((tops[dy] - top) * SCALE) for dy in range(4))
    inv = 1.0 / total
    stats[0, 0:8, :] = top
    stats[0, 8:16, :] = inv
    stat_copy(0, 0, 1).start()
    for d in (1, 3, 2):
        for h in range(2):
            for dc in range(2):
                stat_copy(h, d, dc).start()

    def sums(h, rows_ref, top, inv):
        rows = rows_ref[...]
        for u in range(2):
            span = pl.ds(u * 256, 256)
            s = lax.dot_general(cc[h, span, :], rows, NT, preferred_element_type=F32)
            p = (jnp.exp2((s - top) * SCALE) * inv).astype(BF16)
            w = p.astype(F32)
            cols[h, span, :] += sum(w[:, g * 128 : (g + 1) * 128] for g in range(N // 128))
            acc[h, span, :] += lax.dot_general(p, rows, NN, preferred_element_type=F32)

    def chip_sums(rows, k):
        for h in range(2):
            sums(h, rows, stats[k, 0:1, :], stats[k, 8:9, :])

    def near_sums(k):
        for h in range(2):
            pass_near(h, k).wait_recv()
        lanes = pl.ds(k * PIECE, PIECE)
        for h in range(2):
            order = [slot(h, d, dc) for dc in range(2) for d in (1, 3)]
            top = jnp.concatenate([stats[i, 0:1, lanes] for i in order], axis=1)
            inv = jnp.concatenate([stats[i, 8:9, lanes] for i in order], axis=1)
            sums(h, xn.at[h, k], top, inv)

    def far_sums(h):
        for dy in range(4):
            pass_far(h, dy).wait_recv()
        for dc in range(2):
            k = slot(h, 2, dc)
            sums(h, xf.at[h, dc], stats[k, 0:1, :], stats[k, 8:9, :])

    def take_far(h, dy):
        y_recv(h, dy).wait_recv()
        pass_far(h, dy).start()

    def part(h, q):
        return remote(sb.at[h, q], rb.at[h, q], rs.at[h, q], rr.at[h, q], to_axis(1 - h, q))

    def tail(h, q):
        return jnp.sum(jnp.transpose(cols[h, pl.ds(q * HALF, HALF), :]), axis=0, keepdims=True)

    def send_parts(h):
        for q in (2, 1, 3):
            sb[h, q, 0:HALF, :] = acc[h, pl.ds(q * HALF, HALF), :].astype(BF16)
            w = tail(h, q)
            high = w.astype(BF16).astype(F32)
            row = jnp.concatenate([high, w - high, jnp.zeros((1, D - 2 * HALF), F32)], axis=1)
            sb[h, q, HALF:PART, :] = jnp.broadcast_to(row, (16, D)).astype(BF16)
            part(h, q).start()

    def resp(a, b):
        @pl.loop(a, b)
        def _(j):
            for u in range(2):
                s = lax.dot_general(x_ref[...], cv[j, pl.ds(u * 256, 256), :], NT, preferred_element_type=F32)
                for g in range(2):
                    t = s[:, g * 128 : (g + 1) * 128]
                    lanes = pl.ds(pl.multiple_of(j * CH + u * 256 + g * 128, 128), 128)
                    resp_ref[:, lanes] = (jnp.exp2((t - topc[...]) * SCALE) * invc[...]).astype(BF16)

    take_near(0)
    for h in range(2):
        for q in range(4):
            cc_copy(h, q).wait()
    chip_sums(x_ref, 0)
    for dy in (1, 3, 2):
        y_send(1, dy).start()
    sibling.wait_recv()
    stat_copy(0, 0, 1).wait_recv()
    chip_sums(xs, 1)
    take_near(1)
    start_near(3)
    for h in range(2):
        for d in (1, 2, 3):
            for dc in range(2):
                stat_copy(h, d, dc).wait_recv()
    near_sums(0)
    take_near(2)
    near_sums(1)
    for dy in (1, 3, 2):
        take_far(0, dy)
    near_sums(2)
    take_near(3)
    far_sums(0)
    take_far(1, 1)
    take_far(1, 3)
    near_sums(3)
    send_parts(0)
    take_far(1, 2)
    topc[...] = jnp.transpose(jnp.broadcast_to(stats[0, 0:1, :], (128, N)))
    invc[...] = jnp.transpose(jnp.broadcast_to(stats[0, 8:9, :], (128, N)))
    far_sums(1)
    send_parts(1)
    resp(0, NCH)

    for h in (0, 1):
        total = acc[h, 0:HALF, :]
        w = tail(h, 0)
        for q in (1, 3, 2):
            part(h, q).wait_recv()
            total = total + rb[h, q, 0:HALF, :].astype(F32)
            row = rb[h, q, HALF:PART, :].astype(F32)[0:1, :]
            w = w + row[:, 0:HALF] + row[:, HALF : 2 * HALF]
        numer_ref[pl.ds(h * HALF, HALF), :] = total
        w_ref[:, pl.ds(h * HALF, HALF)] = jnp.broadcast_to(w, (8, HALF))

    sibling.wait_send()
    stat_copy(0, 0, 1).wait_send()
    for h in range(2):
        far(h).wait_send()
        for k in range(4):
            pass_far(h, k).wait_send()
            pass_near(h, k).wait_send()
            for side in range(2):
                near(h, k, side).wait_send()
        for d in (1, 2, 3):
            y_send(h, d).wait_send()
            part(h, d).wait_send()
            for dc in range(2):
                stat_copy(h, d, dc).wait_send()
    for dy in (1, 2, 3):
        ystat_copy(dy).wait_send()


def main_call(embeds, centroids):
    vmem = pl.BlockSpec(memory_space=pltpu.VMEM)
    dma = pltpu.SemaphoreType.DMA
    return pl.pallas_call(
        main_kernel,
        out_shape=[
            jax.ShapeDtypeStruct((N, KL), BF16),
            jax.ShapeDtypeStruct((OWN, D), F32),
            jax.ShapeDtypeStruct((8, OWN), F32),
        ],
        in_specs=[vmem, pl.BlockSpec(memory_space=pl.ANY)],
        out_specs=[vmem] * 3,
        scratch_shapes=[
            pltpu.VMEM((N, D), BF16),
            pltpu.VMEM((2, 4, 4 * PIECE, D), BF16),
            pltpu.VMEM((2, 2, N, D), BF16),
            pltpu.VMEM((NCH, CH, D), BF16),
            pltpu.VMEM((2, 4 * HALF, D), BF16),
            pltpu.VMEM((N, CH), F32),
            pltpu.VMEM((N, CH), F32),
            pltpu.VMEM((N, 128), F32),
            pltpu.VMEM((N, 128), F32),
            pltpu.VMEM((2, 4 * HALF, D), F32),
            pltpu.VMEM((2, 4 * HALF, 128), F32),
            pltpu.VMEM((14, 16, N), F32),
            pltpu.VMEM((4, 16, N), F32),
            pltpu.VMEM((N, 128), F32),
            pltpu.VMEM((N, 128), F32),
            pltpu.VMEM((2, 4, PART, D), BF16),
            pltpu.VMEM((2, 4, PART, D), BF16),
            dma((NCH,)), dma((2, 4)), dma(()), dma(()),
            dma((2, 4, 2)), dma((2, 4, 2)), dma((2,)), dma((2,)), dma((2, 4)), dma((2, 4)),
            dma((2, 4)), dma((2, 4)), dma((2, 4)), dma((2, 4)), dma((14,)), dma((14,)), dma((4,)), dma((4,)),
            dma((2, 4)), dma((2, 4)),
        ],
        compiler_params=pltpu.CompilerParams(
            collective_id=0, has_side_effects=True, vmem_limit_bytes=VMEM_LIMIT
        ),
        cost_estimate=pl.CostEstimate(flops=26_000_000_000, bytes_accessed=22_000_000, transcendentals=13_000_000),
    )(embeds, centroids)


def out_kernel(resp_ref, numer_ref, w_ref, resp_out, numer_out, w_out, sem):
    copies = [
        pltpu.make_async_copy(resp_ref.at[pl.ds(i * 64, 64)], resp_out.at[pl.ds(i * 64, 64)], sem.at[i])
        for i in range(8)
    ]
    copies.append(pltpu.make_async_copy(numer_ref, numer_out, sem.at[8]))
    for copy in copies:
        copy.start()
    w_out[...] = w_ref[0:1, :]
    for copy in copies:
        copy.wait()


def out_call(resp, numer, weights):
    vmem, any_ = pl.BlockSpec(memory_space=pltpu.VMEM), pl.BlockSpec(memory_space=pl.ANY)
    return pl.pallas_call(
        out_kernel,
        out_shape=[
            jax.ShapeDtypeStruct((N, KL), BF16),
            jax.ShapeDtypeStruct((OWN, D), F32),
            jax.ShapeDtypeStruct((1, OWN), F32),
        ],
        in_specs=[vmem] * 3,
        out_specs=[any_, any_, vmem],
        scratch_shapes=[pltpu.SemaphoreType.DMA((9,))],
        compiler_params=pltpu.CompilerParams(vmem_limit_bytes=20 << 20),
    )(resp, numer, weights)


def shards(embeds, centroids):
    resp, numer, weights = out_call(*main_call(embeds, centroids))
    return resp, jnp.reshape(weights, (OWN,)), numer


def solution(mesh):
    return jax.shard_map(
        shards,
        mesh=mesh,
        in_specs=(P("rows", None), P("cent", None)),
        out_specs=(P("rows", "cent"), P(("cent", "rows")), P(("cent", "rows"), None)),
        check_vma=False,
    )
```

time: 224 us -> 65.3 us (0.29)
  blocking collectives: 143 us -> 0 us
  Pallas kernels: 0 us -> 63.2 us
  matrix products: 26.6 us -> 0 us
  waiting for transfers between devices: 16.7 us -> 0 us
  other arithmetic: 16.6 us -> 0 us
  between operations: 14.7 us -> 0.83 us
  local copies, waits for them, and re-layouts: 6.32 us -> 1.13 us
    unnamed x1 -> x0, blocking collectives: 127 us -> none
    pallas_call x0 -> x2, Pallas kernels: none -> 63.2 us  [the longest x1 59 us: main_call(): pl.pallas_call(main_kernel, out_shape=[jax.ShapeDtypeStruct((N, KL), BF16...]
    dot_general x2 -> x0, matrix products: 26.6 us -> none  [the longest x1 14.8 us: shards(): lax.dot_general(embeds, centroids, (((1,), (1,)), ((), ())), preferred_el...]
    reduce_scatter x1 -> x0, waiting for transfers between devices: 16.6 us -> none  [shards(): lax.psum_scatter(term, 'rows', scatter_dimension=0, tiled=True)]
    reduce_sum x2 -> x0, other arithmetic: 16.6 us -> none  [the longest x1 8.62 us: shards(): total = lax.psum(jnp.sum(expo, axis=1), 'cent')]
    pmax x1 -> x0, blocking collectives: 9.53 us -> none  [shards(): peak = lax.pmax(local_peak, 'cent')]
    psum x1 -> x0, blocking collectives: 6 us -> none  [shards(): total = lax.psum(jnp.sum(expo, axis=1), 'cent')]
    unnamed x8 -> x2, local copies, waits for them, and re-layouts: 6.32 us -> 1.13 us
  transfers between devices with their start and end apart: 1 -> 0, of which waited for: 1 -> 0; matrix products, arithmetic and copies ran while one was open for 1% -> 0% of each run, Pallas kernels for 0% -> 0%
where the time goes in v1:
time: 65.3 us; the launch traced here: 65.1 us
  Pallas kernels  63.2 us (97%)
  local copies, waits for them, and re-layouts  1.13 us (2%)
  between operations  0.83 us (1%)
    pallas_call x1, Pallas kernels, main_call(): pl.pallas_call(main_kernel, out_shape=[jax.ShapeDtypeStruct((N, KL), BF16...  59 us
    pallas_call x1, Pallas kernels, out_call(): pl.pallas_call(out_kernel, out_shape=[jax.ShapeDtypeStruct((N, KL), BF16)...  4.16 us

profile of v1, /device:TPU:1, one launch (start us, length us, event | category | flops | bytes accessed | tf_op | source)
XLA Modules:
  0.0 65.1 jit_solution(11004804478092058667)
XLA Ops:
  0.6 0.0 copy-start
  0.6 1.1 %copy-done = bf16[512,768]{1,0:T(8,128)(2,1)S(1)} copy-done((bf16[512,768]{1,0:T(8,128)(2,1)S(1)}, bf16[512,768]{1,0:T(8,128)(2,1)}, u32[]{:S(2)}) %copy-start) | copy-done | bytes 786456
  1.8 59.0 %shard_map.49 = (bf16[512,8192]{1,0:T(8,128)(2,1)S(1)}, f32[256,768]{1,0:T(8,128)S(1)}, f32[8,256]{1,0:T(8,128)S(1)}) custom-call(bf16[512,768]{1,0:T(8,128)(2,1)S(1)} %copy-done, bf16[8192,768]{1,0:T(8,128)(2,1)} %c_hbm.1), custom_call_target="tpu_custom_call" | custom-call | flops 25999998976 | bytes 22000000 | tf_op jit(solution)/shard_map/pallas_call | solution.py:345
  60.8 4.2 %shard_map.50 = (bf16[512,8192]{1,0:T(8,128)(2,1)}, f32[256,768]{1,0:T(8,128)}, f32[1,256]{1,0:T(1,128)}) custom-call(bf16[512,8192]{1,0:T(8,128)(2,1)S(1)} %get-tuple-element.9.resp_ref, f32[256,768]{1,0:T(8,128)S(1)} %get-tuple-element.10.numer_ref, f32[8,256]{1,0:T(8,128)S(1)} %get-tuple-element.11.w_ref), custom_call_target="tpu_custom_call" | custom-call | tf_op jit(solution)/shard_map/pallas_call | solution.py:399
Async XLA Ops:
  0.6 1.1 %copy-start = (bf16[512,768]{1,0:T(8,128)(2,1)S(1)}, bf16[512,768]{1,0:T(8,128)(2,1)}, u32[]{:S(2)}) copy-start(bf16[512,768]{1,0:T(8,128)(2,1)} %x_ref.1) | copy-start | bytes 2359300

commit v2 on v1

--- a/solution.py
+++ b/solution.py
@@ -15,9 +15,8 @@
 NCH = KL // CH
 OWN = 256
 QF = 128
-PIECE = 128
+PIECE = 256
 HALF = 128
-PART = HALF + 16
 VMEM_LIMIT = 40 << 20
 SCALE = 10.0 * math.log2(math.e)
 F32, BF16 = jnp.float32, jnp.bfloat16
@@ -51,8 +50,8 @@
         l_ref[rows, :] = total
 
 
-def slot(h, d, dc):
-    return d * 2 + dc + 6 * h if d else dc
+def slot(h, d):
+    return d + 3 * h if d else 0
 
 
 def to_axis(h, d, dc=0):
@@ -65,8 +64,8 @@
 
 def main_kernel(
     x_ref, c_hbm, resp_ref, numer_ref, w_ref,
-    xs, xn, xf, cv, cc, s0, s1, m_ref, l_ref, acc, cols, stats, ystats, topc, invc, sb, rb,
-    c_sem, cc_sem, own_s, own_r, near_s, near_r, far_s, far_r, ys, yr, pn_s, pn_r, pf_s, pf_r, ss, sr, yss, ysr, rs, rr,
+    xs, xn, xf, cv, cc, s0, s1, m_ref, l_ref, acc, cols, stats, ystats, topc, invc, sb, rb, wsb, wrb,
+    c_sem, cc_sem, own_s, own_r, near_s, near_r, far_s, far_r, ys, yr, pn_s, pn_r, pf_s, pf_r, ss, sr, yss, ysr, rs, rr, ws, wr,
 ):
     z, x, c, y = position()
     def c_copy(j):
@@ -145,14 +144,19 @@
         rows = xf.at[h, 0, quarter(lax.rem(y + 4 - dy, 4))]
         return remote(rows, rows, ys.at[h, dy], yr.at[h, dy], (0, 0, 0, dy))
 
-    def pass_far(h, dy):
-        rows = quarter(lax.rem(y + 4 - dy, 4))
-        return remote(xf.at[h, 0, rows], xf.at[h, 1, rows], pf_s.at[h, dy], pf_r.at[h, dy], (0, 0, 1, 0))
-
-    def stat_copy(h, d, dc):
-        k = slot(h, d, dc)
-        to = to_axis(h, (4 - d) % 4, dc)
-        return remote(stats.at[0], stats.at[k], ss.at[k], sr.at[k], to)
+    def pass_far(h):
+        return remote(xf.at[h, 0], xf.at[h, 1], pf_s.at[h], pf_r.at[h], (0, 0, 1, 0))
+
+    def stat_copy(h, d):
+        k = slot(h, d)
+        return remote(stats.at[0, 0], stats.at[0, k], ss.at[k], sr.at[k], to_axis(h, 4 - d))
+
+    def stat_sibling():
+        return remote(stats.at[0, 0], stats.at[1, 0], ss.at[0], sr.at[0], (0, 0, 1, 0))
+
+    def stat_pass():
+        rows = pl.ds(1, 6)
+        return remote(stats.at[0, rows], stats.at[1, rows], ss.at[7], sr.at[7], (0, 0, 1, 0))
 
     def ystat_copy(dy):
         return remote(ystats.at[0], ystats.at[dy], yss.at[dy], ysr.at[dy], (0, 0, 0, dy))
@@ -178,9 +182,7 @@
     for h in range(2):
         for q in range(4):
             cc_copy(h, q).start()
-    steps(4, 6)
-    start_near(1)
-    steps(6, 7)
+    steps(4, 7)
     c_copy(NCH - 1).wait()
     scores(NCH - 1, s1)
     first_pass(s0, m_ref, l_ref)
@@ -196,24 +198,23 @@
         ystat_copy(dy).start()
     for h in range(2):
         far(h).wait_recv()
-        if h == 0:
-            for dy in (1, 3, 2):
-                y_send(h, dy).start()
-        pass_far(h, 0).start()
-    start_near(2)
+    for dy in (1, 3, 2):
+        y_send(0, dy).start()
+    for h in range(2):
+        for q in range(4):
+            cc_copy(h, q).wait()
     for dy in (1, 2, 3):
         ystat_copy(dy).wait_recv()
     tops = [ystats[dy, 0:8, :] for dy in range(4)]
     top = functools.reduce(jnp.maximum, tops)
     total = sum(ystats[dy, 8:16, :] * jnp.exp2((tops[dy] - top) * SCALE) for dy in range(4))
     inv = 1.0 / total
-    stats[0, 0:8, :] = top
-    stats[0, 8:16, :] = inv
-    stat_copy(0, 0, 1).start()
-    for d in (1, 3, 2):
-        for h in range(2):
-            for dc in range(2):
-                stat_copy(h, d, dc).start()
+    stats[0, 0, 0:8, :] = top
+    stats[0, 0, 8:16, :] = inv
+    stat_sibling().start()
+    for h in range(2):
+        for d in (1, 3, 2):
+            stat_copy(h, d).start()
 
     def sums(h, rows_ref, top, inv):
         rows = rows_ref[...]
@@ -225,45 +226,43 @@
             cols[h, span, :] += sum(w[:, g * 128 : (g + 1) * 128] for g in range(N // 128))
             acc[h, span, :] += lax.dot_general(p, rows, NN, preferred_element_type=F32)
 
-    def chip_sums(rows, k):
+    def chip_sums(rows, dc):
         for h in range(2):
-            sums(h, rows, stats[k, 0:1, :], stats[k, 8:9, :])
-
-    def near_sums(k):
-        for h in range(2):
-            pass_near(h, k).wait_recv()
+            sums(h, rows, stats[dc, 0, 0:1, :], stats[dc, 0, 8:9, :])
+
+    def near_sums(k, dc):
         lanes = pl.ds(k * PIECE, PIECE)
         for h in range(2):
-            order = [slot(h, d, dc) for dc in range(2) for d in (1, 3)]
-            top = jnp.concatenate([stats[i, 0:1, lanes] for i in order], axis=1)
-            inv = jnp.concatenate([stats[i, 8:9, lanes] for i in order], axis=1)
-            sums(h, xn.at[h, k], top, inv)
-
-    def far_sums(h):
-        for dy in range(4):
-            pass_far(h, dy).wait_recv()
-        for dc in range(2):
-            k = slot(h, 2, dc)
-            sums(h, xf.at[h, dc], stats[k, 0:1, :], stats[k, 8:9, :])
-
-    def take_far(h, dy):
-        y_recv(h, dy).wait_recv()
-        pass_far(h, dy).start()
+            order = [slot(h, d) for d in (1, 3)]
+            top = jnp.concatenate([stats[dc, i, 0:1, lanes] for i in order], axis=1)
+            inv = jnp.concatenate([stats[dc, i, 8:9, lanes] for i in order], axis=1)
+            sums(h, xn.at[h, k, pl.ds(dc * N, N)], top, inv)
+
+    def far_sums(h, dc):
+        k = slot(h, 2)
+        sums(h, xf.at[h, dc], stats[dc, k, 0:1, :], stats[dc, k, 8:9, :])
+
+    def take_far(h):
+        for dy in (1, 3, 2):
+            y_recv(h, dy).wait_recv()
+        pass_far(h).start()
 
     def part(h, q):
         return remote(sb.at[h, q], rb.at[h, q], rs.at[h, q], rr.at[h, q], to_axis(1 - h, q))
 
+    def weight(h, q):
+        return remote(wsb.at[h, q], wrb.at[h, q], ws.at[h, q], wr.at[h, q], to_axis(1 - h, q))
+
     def tail(h, q):
         return jnp.sum(jnp.transpose(cols[h, pl.ds(q * HALF, HALF), :]), axis=0, keepdims=True)
 
     def send_parts(h):
         for q in (2, 1, 3):
-            sb[h, q, 0:HALF, :] = acc[h, pl.ds(q * HALF, HALF), :].astype(BF16)
-            w = tail(h, q)
-            high = w.astype(BF16).astype(F32)
-            row = jnp.concatenate([high, w - high, jnp.zeros((1, D - 2 * HALF), F32)], axis=1)
-            sb[h, q, HALF:PART, :] = jnp.broadcast_to(row, (16, D)).astype(BF16)
+            sb[h, q] = acc[h, pl.ds(q * HALF, HALF), :].astype(BF16)
             part(h, q).start()
+        for q in (2, 1, 3):
+            wsb[h, q] = jnp.broadcast_to(tail(h, q), (8, HALF))
+            weight(h, q).start()
 
     def resp(a, b):
         @pl.loop(a, b)
@@ -275,68 +274,77 @@
                     lanes = pl.ds(pl.multiple_of(j * CH + u * 256 + g * 128, 128), 128)
                     resp_ref[:, lanes] = (jnp.exp2((t - topc[...]) * SCALE) * invc[...]).astype(BF16)
 
-    take_near(0)
-    for h in range(2):
-        for q in range(4):
-            cc_copy(h, q).wait()
     chip_sums(x_ref, 0)
     for dy in (1, 3, 2):
         y_send(1, dy).start()
+    start_near(1)
     sibling.wait_recv()
-    stat_copy(0, 0, 1).wait_recv()
+    stat_sibling().wait_recv()
     chip_sums(xs, 1)
+    for h in range(2):
+        for d in (1, 3, 2):
+            stat_copy(h, d).wait_recv()
+    stat_pass().start()
+    topc[...] = jnp.transpose(jnp.broadcast_to(stats[0, 0, 0:1, :], (128, N)))
+    invc[...] = jnp.transpose(jnp.broadcast_to(stats[0, 0, 8:9, :], (128, N)))
+    take_near(0)
+    near_sums(0, 0)
+    stat_pass().wait_recv()
+    for h in range(2):
+        pass_near(h, 0).wait_recv()
+    near_sums(0, 1)
+    take_far(0)
+    far_sums(0, 0)
+    pass_far(0).wait_recv()
+    far_sums(0, 1)
+    sibling.wait_send()
+    stat_sibling().wait_send()
+    stat_pass().wait_send()
+    for h in range(2):
+        far(h).wait_send()
+        pass_near(h, 0).wait_send()
+        for side in range(2):
+            near(h, 0, side).wait_send()
+        for d in (1, 2, 3):
+            stat_copy(h, d).wait_send()
+    for dy in (1, 2, 3):
+        ystat_copy(dy).wait_send()
+        y_send(0, dy).wait_send()
     take_near(1)
-    start_near(3)
-    for h in range(2):
-        for d in (1, 2, 3):
-            for dc in range(2):
-                stat_copy(h, d, dc).wait_recv()
-    near_sums(0)
-    take_near(2)
-    near_sums(1)
-    for dy in (1, 3, 2):
-        take_far(0, dy)
-    near_sums(2)
-    take_near(3)
-    far_sums(0)
-    take_far(1, 1)
-    take_far(1, 3)
-    near_sums(3)
+    near_sums(1, 0)
+    for h in range(2):
+        pass_near(h, 1).wait_recv()
+    near_sums(1, 1)
+    take_far(1)
     send_parts(0)
-    take_far(1, 2)
-    topc[...] = jnp.transpose(jnp.broadcast_to(stats[0, 0:1, :], (128, N)))
-    invc[...] = jnp.transpose(jnp.broadcast_to(stats[0, 8:9, :], (128, N)))
-    far_sums(1)
+    far_sums(1, 0)
+    pass_far(1).wait_recv()
+    far_sums(1, 1)
     send_parts(1)
     resp(0, NCH)
+    for h in range(2):
+        pass_near(h, 1).wait_send()
+        for side in range(2):
+            near(h, 1, side).wait_send()
+        pass_far(h).wait_send()
+    for dy in (1, 2, 3):
+        y_send(1, dy).wait_send()
 
     for h in (0, 1):
         total = acc[h, 0:HALF, :]
         w = tail(h, 0)
         for q in (1, 3, 2):
             part(h, q).wait_recv()
-            total = total + rb[h, q, 0:HALF, :].astype(F32)
-            row = rb[h, q, HALF:PART, :].astype(F32)[0:1, :]
-            w = w + row[:, 0:HALF] + row[:, HALF : 2 * HALF]
+            total = total + rb[h, q].astype(F32)
+            weight(h, q).wait_recv()
+            w = w + wrb[h, q, 0:1, :]
         numer_ref[pl.ds(h * HALF, HALF), :] = total
         w_ref[:, pl.ds(h * HALF, HALF)] = jnp.broadcast_to(w, (8, HALF))
 
-    sibling.wait_send()
-    stat_copy(0, 0, 1).wait_send()
-    for h in range(2):
-        far(h).wait_send()
-        for k in range(4):
-            pass_far(h, k).wait_send()
-            pass_near(h, k).wait_send()
-            for side in range(2):
-                near(h, k, side).wait_send()
-        for d in (1, 2, 3):
-            y_send(h, d).wait_send()
-            part(h, d).wait_send()
-            for dc in range(2):
-                stat_copy(h, d, dc).wait_send()
-    for dy in (1, 2, 3):
-        ystat_copy(dy).wait_send()
+    for h in range(2):
+        for q in (1, 2, 3):
+            part(h, q).wait_send()
+            weight(h, q).wait_send()
 
 
 def main_call(embeds, centroids):
@@ -353,7 +361,7 @@
         out_specs=[vmem] * 3,
         scratch_shapes=[
             pltpu.VMEM((N, D), BF16),
-            pltpu.VMEM((2, 4, 4 * PIECE, D), BF16),
+            pltpu.VMEM((2, N // PIECE, 4 * PIECE, D), BF16),
             pltpu.VMEM((2, 2, N, D), BF16),
             pltpu.VMEM((NCH, CH, D), BF16),
             pltpu.VMEM((2, 4 * HALF, D), BF16),
@@ -363,16 +371,18 @@
             pltpu.VMEM((N, 128), F32),
             pltpu.VMEM((2, 4 * HALF, D), F32),
             pltpu.VMEM((2, 4 * HALF, 128), F32),
-            pltpu.VMEM((14, 16, N), F32),
+            pltpu.VMEM((2, 7, 16, N), F32),
             pltpu.VMEM((4, 16, N), F32),
             pltpu.VMEM((N, 128), F32),
             pltpu.VMEM((N, 128), F32),
-            pltpu.VMEM((2, 4, PART, D), BF16),
-            pltpu.VMEM((2, 4, PART, D), BF16),
+            pltpu.VMEM((2, 4, HALF, D), BF16),
+            pltpu.VMEM((2, 4, HALF, D), BF16),
+            pltpu.VMEM((2, 4, 8, HALF), F32),
+            pltpu.VMEM((2, 4, 8, HALF), F32),
             dma((NCH,)), dma((2, 4)), dma(()), dma(()),
             dma((2, 4, 2)), dma((2, 4, 2)), dma((2,)), dma((2,)), dma((2, 4)), dma((2, 4)),
-            dma((2, 4)), dma((2, 4)), dma((2, 4)), dma((2, 4)), dma((14,)), dma((14,)), dma((4,)), dma((4,)),
-            dma((2, 4)), dma((2, 4)),
+            dma((2, 4)), dma((2, 4)), dma((2,)), dma((2,)), dma((8,)), dma((8,)), dma((4,)), dma((4,)),
+            dma((2, 4)), dma((2, 4)), dma((2, 4)), dma((2, 4)),
         ],
         compiler_params=pltpu.CompilerParams(
             collective_id=0, has_side_effects=True, vmem_limit_bytes=VMEM_LIMIT

time: 65.3 us -> 62.3 us (0.954)
  Pallas kernels: 63.2 us -> 60.2 us
    pallas_call x1, Pallas kernels: 59 us -> 56 us  [main_call(): pl.pallas_call(main_kernel, out_shape=[jax.ShapeDtypeStruct((N, KL), BF16...]
where the time goes in v2:
time: 62.3 us; the launch traced here: 62.1 us
  Pallas kernels  60.2 us (97%)
  local copies, waits for them, and re-layouts  1.13 us (2%)
  between operations  0.83 us (1%)
    pallas_call x1, Pallas kernels, main_call(): pl.pallas_call(main_kernel, out_shape=[jax.ShapeDtypeStruct((N, KL), BF16...  56 us
    pallas_call x1, Pallas kernels, out_call(): pl.pallas_call(out_kernel, out_shape=[jax.ShapeDtypeStruct((N, KL), BF16)...  4.16 us

profile of v2, /device:TPU:1, one launch (start us, length us, event | category | flops | bytes accessed | tf_op | source)
XLA Modules:
  0.0 62.1 jit_solution(11465752355484623418)
XLA Ops:
  0.6 0.0 copy-start
  0.6 1.1 %copy-done = bf16[512,768]{1,0:T(8,128)(2,1)S(1)} copy-done((bf16[512,768]{1,0:T(8,128)(2,1)S(1)}, bf16[512,768]{1,0:T(8,128)(2,1)}, u32[]{:S(2)}) %copy-start) | copy-done | bytes 786456
  1.8 56.0 %shard_map.49 = (bf16[512,8192]{1,0:T(8,128)(2,1)S(1)}, f32[256,768]{1,0:T(8,128)S(1)}, f32[8,256]{1,0:T(8,128)S(1)}) custom-call(bf16[512,768]{1,0:T(8,128)(2,1)S(1)} %copy-done, bf16[8192,768]{1,0:T(8,128)(2,1)} %c_hbm.1), custom_call_target="tpu_custom_call" | custom-call | flops 25999998976 | bytes 22000000 | tf_op jit(solution)/shard_map/pallas_call | solution.py:353
  57.8 4.2 %shard_map.50 = (bf16[512,8192]{1,0:T(8,128)(2,1)}, f32[256,768]{1,0:T(8,128)}, f32[1,256]{1,0:T(1,128)}) custom-call(bf16[512,8192]{1,0:T(8,128)(2,1)S(1)} %get-tuple-element.9.resp_ref, f32[256,768]{1,0:T(8,128)S(1)} %get-tuple-element.10.numer_ref, f32[8,256]{1,0:T(8,128)S(1)} %get-tuple-element.11.w_ref), custom_call_target="tpu_custom_call" | custom-call | tf_op jit(solution)/shard_map/pallas_call | solution.py:409
Async XLA Ops:
  0.6 1.1 %copy-start = (bf16[512,768]{1,0:T(8,128)(2,1)S(1)}, bf16[512,768]{1,0:T(8,128)(2,1)}, u32[]{:S(2)}) copy-start(bf16[512,768]{1,0:T(8,128)(2,1)} %x_ref.1) | copy-start | bytes 2359300

commit v3 on v2

--- a/solution.py
+++ b/solution.py
@@ -58,7 +58,7 @@
     return (0, d, dc, 0) if h == 0 else (d, 0, dc, 0)
 
 
-PEERS = [(0, 0, 1, 0)] + [to_axis(h, d, dc) for h in range(2) for d in (1, 2, 3) for dc in range(2)]
+PEERS = [(0, 0, 1, 0)] + [to_axis(h, d) for h in range(2) for d in (1, 2, 3)]
 YPEERS = [(0, 0, 0, dy) for dy in (1, 2, 3)]
 
 
@@ -78,11 +78,12 @@
             c_hbm.at[pl.ds(start, HALF)], cc.at[h, pl.ds(q * HALF, HALF)], cc_sem.at[h, q]
         )
 
-    for j in range(AHEAD):
-        c_copy(j).start()
+    c_copy(0).start()
     bar = pltpu.get_barrier_semaphore()
     for p in PEERS + YPEERS:
         pl.semaphore_signal(bar, inc=1, device_id=device(*p), device_id_type=MESH)
+    for j in range(1, AHEAD):
+        c_copy(j).start()
     m_ref[...] = jnp.full(m_ref.shape, -3e38, F32)
     l_ref[...] = jnp.zeros(l_ref.shape, F32)
     acc[...] = jnp.zeros(acc.shape, F32)
@@ -265,9 +266,9 @@
             weight(h, q).start()
 
     def resp(a, b):
-        @pl.loop(a, b)
-        def _(j):
-            for u in range(2):
+        @pl.loop(a, b, step=4)
+        def _(first):
+            for j, u in [(first + i, u) for i in range(4) for u in range(2)]:
                 s = lax.dot_general(x_ref[...], cv[j, pl.ds(u * 256, 256), :], NT, preferred_element_type=F32)
                 for g in range(2):
                     t = s[:, g * 128 : (g + 1) * 128]

time: 62.3 us -> 61.4 us (0.986)
  Pallas kernels: 60.2 us -> 59.3 us
    pallas_call x1, Pallas kernels: 56 us -> 55.1 us  [main_call(): pl.pallas_call(main_kernel, out_shape=[jax.ShapeDtypeStruct((N, KL), BF16...]
where the time goes in v3:
time: 61.4 us; the launch traced here: 61.3 us
  Pallas kernels  59.3 us (97%)
  local copies, waits for them, and re-layouts  1.13 us (2%)
  between operations  0.83 us (1%)
    pallas_call x1, Pallas kernels, main_call(): pl.pallas_call(main_kernel, out_shape=[jax.ShapeDtypeStruct((N, KL), BF16...  55.1 us
    pallas_call x1, Pallas kernels, out_call(): pl.pallas_call(out_kernel, out_shape=[jax.ShapeDtypeStruct((N, KL), BF16)...  4.16 us

profile of v3, /device:TPU:1, one launch (start us, length us, event | category | flops | bytes accessed | tf_op | source)
XLA Modules:
  0.0 61.3 jit_solution(11849923350899886031)
XLA Ops:
  0.6 0.0 copy-start
  0.6 1.1 %copy-done = bf16[512,768]{1,0:T(8,128)(2,1)S(1)} copy-done((bf16[512,768]{1,0:T(8,128)(2,1)S(1)}, bf16[512,768]{1,0:T(8,128)(2,1)}, u32[]{:S(2)}) %copy-start) | copy-done | bytes 786456
  1.8 55.1 %shard_map.49 = (bf16[512,8192]{1,0:T(8,128)(2,1)S(1)}, f32[256,768]{1,0:T(8,128)S(1)}, f32[8,256]{1,0:T(8,128)S(1)}) custom-call(bf16[512,768]{1,0:T(8,128)(2,1)S(1)} %copy-done, bf16[8192,768]{1,0:T(8,128)(2,1)} %c_hbm.1), custom_call_target="tpu_custom_call" | custom-call | flops 25999998976 | bytes 22000000 | tf_op jit(solution)/shard_map/pallas_call | solution.py:354
  56.9 4.2 %shard_map.50 = (bf16[512,8192]{1,0:T(8,128)(2,1)}, f32[256,768]{1,0:T(8,128)}, f32[1,256]{1,0:T(1,128)}) custom-call(bf16[512,8192]{1,0:T(8,128)(2,1)S(1)} %get-tuple-element.9.resp_ref, f32[256,768]{1,0:T(8,128)S(1)} %get-tuple-element.10.numer_ref, f32[8,256]{1,0:T(8,128)S(1)} %get-tuple-element.11.w_ref), custom_call_target="tpu_custom_call" | custom-call | tf_op jit(solution)/shard_map/pallas_call | solution.py:410
Async XLA Ops:
  0.6 1.1 %copy-start = (bf16[512,768]{1,0:T(8,128)(2,1)S(1)}, bf16[512,768]{1,0:T(8,128)(2,1)}, u32[]{:S(2)}) copy-start(bf16[512,768]{1,0:T(8,128)(2,1)} %x_ref.1) | copy-start | bytes 2359300

commit v4 on v3

--- a/solution.py
+++ b/solution.py
@@ -217,9 +217,9 @@
         for d in (1, 3, 2):
             stat_copy(h, d).start()
 
-    def sums(h, rows_ref, top, inv):
+    def sums(h, rows_ref, top, inv, units=(0, 1)):
         rows = rows_ref[...]
-        for u in range(2):
+        for u in units:
             span = pl.ds(u * 256, 256)
             s = lax.dot_general(cc[h, span, :], rows, NT, preferred_element_type=F32)
             p = (jnp.exp2((s - top) * SCALE) * inv).astype(BF16)
@@ -239,9 +239,9 @@
             inv = jnp.concatenate([stats[dc, i, 8:9, lanes] for i in order], axis=1)
             sums(h, xn.at[h, k, pl.ds(dc * N, N)], top, inv)
 
-    def far_sums(h, dc):
+    def far_sums(h, dc, units=(0, 1)):
         k = slot(h, 2)
-        sums(h, xf.at[h, dc], stats[dc, k, 0:1, :], stats[dc, k, 8:9, :])
+        sums(h, xf.at[h, dc], stats[dc, k, 0:1, :], stats[dc, k, 8:9, :], units)
 
     def take_far(h):
         for dy in (1, 3, 2):
@@ -257,11 +257,11 @@
     def tail(h, q):
         return jnp.sum(jnp.transpose(cols[h, pl.ds(q * HALF, HALF), :]), axis=0, keepdims=True)
 
-    def send_parts(h):
-        for q in (2, 1, 3):
+    def send_parts(h, owners=(2, 1, 3)):
+        for q in owners:
             sb[h, q] = acc[h, pl.ds(q * HALF, HALF), :].astype(BF16)
             part(h, q).start()
-        for q in (2, 1, 3):
+        for q in owners:
             wsb[h, q] = jnp.broadcast_to(tail(h, q), (8, HALF))
             weight(h, q).start()
 
@@ -320,8 +320,10 @@
     send_parts(0)
     far_sums(1, 0)
     pass_far(1).wait_recv()
-    far_sums(1, 1)
-    send_parts(1)
+    far_sums(1, 1, (1,))
+    send_parts(1, (2, 3))
+    far_sums(1, 1, (0,))
+    send_parts(1, (1,))
     resp(0, NCH)
     for h in range(2):
         pass_near(h, 1).wait_send()

time: 61.4 us -> 61.5 us (level)
  no operation moved by 1% of the time
where the time goes in v4:
time: 61.5 us; the launch traced here: 61.3 us
  Pallas kernels  59.3 us (96%)
  local copies, waits for them, and re-layouts  1.13 us (2%)
  between operations  0.83 us (1%)
    pallas_call x1, Pallas kernels, main_call(): pl.pallas_call(main_kernel, out_shape=[jax.ShapeDtypeStruct((N, KL), BF16...  55.2 us
    pallas_call x1, Pallas kernels, out_call(): pl.pallas_call(out_kernel, out_shape=[jax.ShapeDtypeStruct((N, KL), BF16)...  4.16 us

profile of v4, /device:TPU:1, one launch (start us, length us, event | category | flops | bytes accessed | tf_op | source)
XLA Modules:
  0.0 61.3 jit_solution(7511083684385229945)
XLA Ops:
  0.6 0.0 copy-start
  0.6 1.1 %copy-done = bf16[512,768]{1,0:T(8,128)(2,1)S(1)} copy-done((bf16[512,768]{1,0:T(8,128)(2,1)S(1)}, bf16[512,768]{1,0:T(8,128)(2,1)}, u32[]{:S(2)}) %copy-start) | copy-done | bytes 786456
  1.8 55.2 %shard_map.49 = (bf16[512,8192]{1,0:T(8,128)(2,1)S(1)}, f32[256,768]{1,0:T(8,128)S(1)}, f32[8,256]{1,0:T(8,128)S(1)}) custom-call(bf16[512,768]{1,0:T(8,128)(2,1)S(1)} %copy-done, bf16[8192,768]{1,0:T(8,128)(2,1)} %c_hbm.1), custom_call_target="tpu_custom_call" | custom-call | flops 25999998976 | bytes 22000000 | tf_op jit(solution)/shard_map/pallas_call | solution.py:356
  56.9 4.2 %shard_map.50 = (bf16[512,8192]{1,0:T(8,128)(2,1)}, f32[256,768]{1,0:T(8,128)}, f32[1,256]{1,0:T(1,128)}) custom-call(bf16[512,8192]{1,0:T(8,128)(2,1)S(1)} %get-tuple-element.9.resp_ref, f32[256,768]{1,0:T(8,128)S(1)} %get-tuple-element.10.numer_ref, f32[8,256]{1,0:T(8,128)S(1)} %get-tuple-element.11.w_ref), custom_call_target="tpu_custom_call" | custom-call | tf_op jit(solution)/shard_map/pallas_call | solution.py:412
Async XLA Ops:
  0.6 1.1 %copy-start = (bf16[512,768]{1,0:T(8,128)(2,1)S(1)}, bf16[512,768]{1,0:T(8,128)(2,1)}, u32[]{:S(2)}) copy-start(bf16[512,768]{1,0:T(8,128)(2,1)} %x_ref.1) | copy-start | bytes 2359300
